TPU v7x, 32 devices: a whole 2x2x4 slice. The times are simulated.
32 devices in a mesh: group: 8 (over y, x, core), blk: 4 (over z).
Axes of the slice: x: 2, y: 2, z: 4, core: 2. Of those that a mesh axis runs over, the one named last changes fastest.
Arguments:
- queries: bfloat16 [8192, 1024], P(('group', 'blk')), may hold values from -6 to 6
- keys: bfloat16 [8192, 1024], P(('group', 'blk')), may hold values from -6 to 6
- values: bfloat16 [8192, 1024], P(('group', 'blk')), may hold values from -6 to 6
- out_grad: bfloat16 [8192, 1024], P(('group', 'blk')), may hold values from -6 to 6
- send_rows: int32 [32, 32, 16], P(('group', 'blk')), may hold values from 0 to 256, as said below
- recv_slots: int32 [32, 256], P(('group', 'blk')), may hold values from 0 to 511, as said below
- scene_frames: int32 [8, 4], P('group', 'blk'), may hold values from 0 to 1, never falling along the last dimension, each value on 1 to 3 neighbouring positions
Outputs:
- query_grad: bfloat16 [8192, 1024], P(('group', 'blk'))
- key_grad: bfloat16 [8192, 1024], P(('group', 'blk'))
- value_grad: bfloat16 [8192, 1024], P(('group', 'blk'))
Inputs may be any that keep to these rules, and one draw needn't show every extreme that they name: `send_rows`: entry [s, e, c] is a row of device s that goes to slot c of its message to device e, or 256 for an empty slot. Every row of every device is named exactly once; each message carries a run of consecutive rows of its source, in order, and the messages of one source follow one another in order of target; filled slots come first in each message; each message holds 0, 8 or 16 rows, some exactly 16; every device receives exactly 256 rows in all. `recv_slots`: row j of device e takes received slot s * 16 + c (message of device s, slot c), which is filled; each filled slot is taken once, in order of source device and then of slot. `scene_frames`: scene numbers never fall along a group's frames; each scene spans 1 to 3 frames.
All inputs are finite; a program needn't handle non-finite values.
Results may differ from a plain program's by a relative error of at most 0.012.
The roundings to bfloat16 on the way count: a program that leaves them out, or rounds other values in their place, can miss the bound.
Values may be sent and summed in bfloat16 or wider, within the bound.
A program may use at most 128 MiB of HBM per device.

v0:
```python
import jax
import jax.numpy as jnp
from jax import lax
from jax.sharding import PartitionSpec as P

HEADS = 16
HEAD_DIM = 64
FRAME_TOK = 256


LOW_SCORE = -1e30


def shifted(block, axis, distance):
    devices = range(lax.axis_size(axis))
    route = [((i - distance) % len(devices), i) for i in devices]
    return lax.ppermute(block, axis, route)


def split_heads(array):
    return array.reshape(array.shape[0], HEADS, HEAD_DIM)


def block_terms(
    query_heads, grad_heads, query_ids, log_norm, row_dot, key_heads, value_heads, key_ids
):
    scale = HEAD_DIM ** (-0.5)
    in_scene = (query_ids[:, None] == key_ids[None, :])[None]
    scores = jnp.where(
        in_scene,
        jnp.einsum("qhd,khd->hqk", query_heads, key_heads, preferred_element_type=jnp.float32)
        * scale,
        LOW_SCORE,
    )
    weights = jnp.where(in_scene, jnp.exp(scores - log_norm[:, :, None]), 0.0)
    weight_grad = jnp.einsum(
        "qhd,khd->hqk", grad_heads, value_heads, preferred_element_type=jnp.float32
    )
    score_half = (weights * (weight_grad - row_dot[:, :, None]) * scale).astype(jnp.bfloat16)
    return (weights.astype(jnp.bfloat16), score_half)


def shards(queries, keys, values, out_grad, send_rows, recv_slots, scene_frames):
    send_plan = send_rows[0]
    recv_plan = recv_slots[0]
    row_count = queries.shape[0]
    feature_width = queries.shape[1]

    def pack_rows(array):
        return jnp.take(array, send_plan, axis=0, mode="fill", fill_value=0)

    inbound = (
        lax.all_to_all(
            pack_rows(queries), ("group", "blk"), split_axis=0, concat_axis=0, tiled=True
        ),
        lax.all_to_all(pack_rows(keys), ("group", "blk"), split_axis=0, concat_axis=0, tiled=True),
        lax.all_to_all(
            pack_rows(values), ("group", "blk"), split_axis=0, concat_axis=0, tiled=True
        ),
        lax.all_to_all(
            pack_rows(out_grad), ("group", "blk"), split_axis=0, concat_axis=0, tiled=True
        ),
    )

    def place_rows(array):
        return jnp.take(array.reshape(-1, feature_width), recv_plan, axis=0)

    query_rows = place_rows(inbound[0])
    key_rows = place_rows(inbound[1])
    value_rows = place_rows(inbound[2])
    grad_rows = place_rows(inbound[3])
    scene_ids = jnp.repeat(scene_frames[0], FRAME_TOK)
    query_heads = split_heads(query_rows)
    grad_heads = split_heads(grad_rows)
    head_count = query_heads.shape[1]
    scale = HEAD_DIM ** (-0.5)
    run_max = jnp.full((head_count, row_count), LOW_SCORE, jnp.float32)
    key_piece = lax.all_gather(key_rows, "blk", axis=0, tiled=True)
    value_piece = lax.all_gather(value_rows, "blk", axis=0, tiled=True)
    key_ids = lax.all_gather(scene_ids, "blk", axis=0, tiled=True)
    in_scene = (scene_ids[:, None] == key_ids[None, :])[None]
    scores = jnp.where(
        in_scene,
        jnp.einsum(
            "qhd,khd->hqk", query_heads, split_heads(key_piece), preferred_element_type=jnp.float32
        )
        * scale,
        LOW_SCORE,
    )
    weight_grad = jnp.einsum(
        "qhd,khd->hqk", grad_heads, split_heads(value_piece), preferred_element_type=jnp.float32
    )
    new_max = jnp.maximum(run_max, jnp.max(scores, axis=2))
    weights = jnp.where(in_scene, jnp.exp(scores - new_max[:, :, None]), 0.0)
    run_sum = jnp.sum(weights, axis=2)
    run_dot = jnp.sum(weights * weight_grad, axis=2)
    log_norm = new_max + jnp.log(run_sum)
    row_dot = run_dot / run_sum
    zero_rows = jnp.zeros((row_count, feature_width), jnp.float32)

    def cycle_block(accums, block_in):
        piece_keys, piece_values, key_ids = block_in
        weight_half, score_half = block_terms(
            query_heads, grad_heads, scene_ids, log_norm, row_dot, piece_keys, piece_values, key_ids
        )
        return (
            accums[0]
            + jnp.einsum(
                "hqk,qhd->khd", score_half, query_heads, preferred_element_type=jnp.float32
            ).reshape(row_count, feature_width),
            accums[1]
            + jnp.einsum(
                "hqk,qhd->khd", weight_half, grad_heads, preferred_element_type=jnp.float32
            ).reshape(row_count, feature_width),
            accums[2]
            + jnp.einsum(
                "hqk,khd->qhd", score_half, piece_keys, preferred_element_type=jnp.float32
            ).reshape(row_count, feature_width),
        )

    def cycle_turn(turn_index, cycle_state):
        key_piece, value_piece, key_ids, key_acc, value_acc, query_acc = cycle_state
        block_in = (split_heads(key_piece), split_heads(value_piece), key_ids)
        key_acc, value_acc, query_acc = cycle_block((key_acc, value_acc, query_acc), block_in)
        key_piece, value_piece, key_ids = shifted((key_piece, value_piece, key_ids), "blk", 1)
        key_acc, value_acc = shifted((key_acc, value_acc), "blk", 1)
        return (key_piece, value_piece, key_ids, key_acc, value_acc, query_acc)

    final_state = lax.fori_loop(
        0,
        lax.axis_size("blk"),
        cycle_turn,
        (key_rows, value_rows, scene_ids, zero_rows, zero_rows, zero_rows),
    )
    key_grad = final_state[3]
    value_grad = final_state[4]
    query_grad = final_state[5]

    def unpack_rows(array):
        buffer = (
            jnp.zeros((send_plan.size, feature_width), jnp.bfloat16)
            .at[recv_plan]
            .set(array.astype(jnp.bfloat16))
        )
        return buffer.reshape(send_plan.shape[0], send_plan.shape[1], feature_width)

    outbound = (
        lax.all_to_all(
            unpack_rows(query_grad), ("group", "blk"), split_axis=0, concat_axis=0, tiled=True
        ),
        lax.all_to_all(
            unpack_rows(key_grad), ("group", "blk"), split_axis=0, concat_axis=0, tiled=True
        ),
        lax.all_to_all(
            unpack_rows(value_grad), ("group", "blk"), split_axis=0, concat_axis=0, tiled=True
        ),
    )

    def restore_rows(array):
        return (
            jnp.zeros((row_count, feature_width), jnp.bfloat16)
            .at[send_plan.reshape(-1)]
            .set(array.reshape(-1, feature_width), mode="drop")
        )

    return (restore_rows(outbound[0]), restore_rows(outbound[1]), restore_rows(outbound[2]))


def solution(mesh):
    placed = (
        P(("group", "blk"), None),
        P(("group", "blk"), None),
        P(("group", "blk"), None),
        P(("group", "blk"), None),
        P(("group", "blk"), None, None),
        P(("group", "blk"), None),
        P("group", "blk"),
    )
    return jax.shard_map(
        shards,
        mesh=mesh,
        in_specs=placed,
        out_specs=(P(("group", "blk"), None), P(("group", "blk"), None), P(("group", "blk"), None)),
        check_vma=False,
    )
```

profile of v0, /device:TPU:1, one launch (start us, length us, event | category | flops | bytes accessed | tf_op | source)
XLA Modules:
  0.0 679.2 jit_solution(7475135452152744829)
XLA Ops:
  21.5 33.2 %all_to_all.35 = bf16[32,16,1024]{2,1,0:T(8,128)(2,1)S(1)} all-to-all(bf16[32,16,1024]{2,1,0:T(8,128)(2,1)S(1)} %get-tuple-element.177), channel_id=1, replica_groups=mesh['group'=8,'blk'=4] {'group','blk'}, dimensions={0} | all-to-all | bytes 2097152 | tf_op jit(solution)/shard_map/all_to_all | solution.py:57
  54.8 29.4 %all_to_all.36 = bf16[32,16,1024]{2,1,0:T(8,128)(2,1)} all-to-all(bf16[32,16,1024]{2,1,0:T(8,128)(2,1)S(1)} %get-tuple-element.178), channel_id=1, replica_groups=mesh['group'=8,'blk'=4] {'group','blk'}, dimensions={0} | all-to-all | bytes 2097152 | tf_op jit(solution)/shard_map/all_to_all | solution.py:53
  84.2 29.4 %all_to_all.37 = bf16[32,16,1024]{2,1,0:T(8,128)(2,1)} all-to-all(bf16[32,16,1024]{2,1,0:T(8,128)(2,1)S(1)} %get-tuple-element.176), channel_id=1, replica_groups=mesh['group'=8,'blk'=4] {'group','blk'}, dimensions={0} | all-to-all | bytes 2097152 | tf_op jit(solution)/shard_map/all_to_all | solution.py:60
  123.0 20.1 %all-to-all-done = bf16[32,16,1024]{2,1,0:T(8,128)(2,1)S(1)} async-done(((bf16[32,16,1024]{2,1,0:T(8,128)(2,1)}), bf16[32,16,1024]{2,1,0:T(8,128)(2,1)S(1)}, u32[]{:S(2)}, u32[]{:S(2)}) %all-to-all-start) | async-done | bytes 1048608 | tf_op jit(solution)/shard_map/all_to_all | solution.py:56
  147.0 6.3 all-gather
  158.6 31.2 %all-gather.4.cloned.1.call-done = bf16[1024,1024]{1,0:T(8,128)(2,1)} async-done(((bf16[256,1024]{1,0:T(8,128)(2,1)}), bf16[1024,1024]{1,0:T(8,128)(2,1)}) %all-gather.4.cloned.1.call-update) | async-done | bytes 2097168 | tf_op jit(solution)/shard_map/all_gather | solution.py:78
  195.2 6.1 copy-done.5
  201.3 4.5 fusion.10
  205.8 31.0 %all-gather.6.cloned.1.call-done = bf16[1024,1024]{1,0:T(8,128)(2,1)} async-done(((bf16[256,1024]{1,0:T(8,128)(2,1)}), bf16[1024,1024]{1,0:T(8,128)(2,1)}) %all-gather.6.cloned.1.call-update) | async-done | bytes 2097168 | tf_op jit(solution)/shard_map/all_gather | solution.py:79
  239.6 9.6 %multiply_reduce_fusion = f32[16,256]{1,0:T(8,128)S(1)} fusion(f32[16,256,1024]{2,1,0:T(8,128)} %copy-done.5, bf16[256,16,64]{0,2,1:T(8,128)(2,1)} %bitcast.16, bf16[1024,16,64]{0,2,1:T(8,128)(2,1)S(1)} %bitcast.99, f32[16,256]{1,0:T(8,128)S(1)} %broadcast_maximum_fusion, pred[1024]{0:T(1024)(128)(4,1)S(1)} %reshape.320), kind=kOutput, calls=%fused_computation.27 | convolution fusion | flops 562032640 | bytes 19432448 | tf_op jit(solution)/shard_map/qhd,khd->hqk/dot_general | solution.py:90
  251.4 320.2 %while.21 = (s32[]{:T(128)}, bf16[256,1024]{0,1:T(8,128)(2,1)}, bf16[256,1024]{0,1:T(8,128)(2,1)}, s32[256]{0:T(256)S(1)}, f32[256,1024]{0,1:T(8,128)}, /*index=...) while((s32[]{:T(128)}, bf16[256,1024]{0,1:T(8,128)(2,1)}, ...), condition=%wide.region_4.7_spmd.clone, body=%wide.region_3.6_spmd.clone.sunk | while | flops 685768960 | bytes 49864792 | solution.py:129
  272.0 60.8 %collective-permute-done.2 = s32[256]{0:T(256)S(1)} collective-permute-done((s32[256]{0:T(256)S(1)}, s32[256]{0:T(256)S(1)}, u32[]{:S(2)}, u32[]{:S(2)}) %collective-permute-start.2) | collective-permute-done | bytes 1056 | tf_op jit(solution)/shard_map/while/body/eval_jaxpr/ppermute | solution.py:17
  347.7 3.7 collective-permute-start.1
  354.6 58.7 %collective-permute-done.2 = s32[256]{0:T(256)S(1)} collective-permute-done((s32[256]{0:T(256)S(1)}, s32[256]{0:T(256)S(1)}, u32[]{:S(2)}, u32[]{:S(2)}) %collective-permute-start.2) | collective-permute-done | bytes 1056 | tf_op jit(solution)/shard_map/while/body/eval_jaxpr/ppermute | solution.py:17
  428.1 3.8 collective-permute-start.1
  435.1 57.8 %collective-permute-done.2 = s32[256]{0:T(256)S(1)} collective-permute-done((s32[256]{0:T(256)S(1)}, s32[256]{0:T(256)S(1)}, u32[]{:S(2)}, u32[]{:S(2)}) %collective-permute-start.2) | collective-permute-done | bytes 1056 | tf_op jit(solution)/shard_map/while/body/eval_jaxpr/ppermute | solution.py:17
  507.6 3.8 collective-permute-start.1
  514.7 56.9 %collective-permute-done.2 = s32[256]{0:T(256)S(1)} collective-permute-done((s32[256]{0:T(256)S(1)}, s32[256]{0:T(256)S(1)}, u32[]{:S(2)}, u32[]{:S(2)}) %collective-permute-start.2) | collective-permute-done | bytes 1056 | tf_op jit(solution)/shard_map/while/body/eval_jaxpr/ppermute | solution.py:17
  576.0 6.8 all-to-all-start.5
  586.9 22.2 %all-to-all-done.5 = bf16[32,16,1024]{2,1,0:T(8,128)(2,1)S(1)} async-done(((bf16[32,16,1024]{2,1,0:T(8,128)(2,1)}), bf16[32,16,1024]{2,1,0:T(8,128)(2,1)S(1)}, u32[]{:S(2)}, u32[]{:S(2)}) %all-to-all-start.5) | async-done | bytes 1048608 | tf_op jit(solution)/shard_map/all_to_all | solution.py:151
  617.8 20.8 %all-to-all-done.6 = bf16[32,16,1024]{2,1,0:T(8,128)(2,1)S(1)} async-done(((bf16[32,16,1024]{2,1,0:T(8,128)(2,1)}), bf16[32,16,1024]{2,1,0:T(8,128)(2,1)S(1)}, u32[]{:S(2)}, u32[]{:S(2)}) %all-to-all-start.6) | async-done | bytes 1048608 | tf_op jit(solution)/shard_map/all_to_all | solution.py:154
  642.0 3.4 scatter_custom_fusion.3
  648.9 19.3 %all-to-all-done.4 = bf16[32,16,1024]{2,1,0:T(8,128)(2,1)} async-done(((bf16[32,16,1024]{2,1,0:T(8,128)(2,1)}), bf16[32,16,1024]{2,1,0:T(8,128)(2,1)}, u32[]{:S(2)}, u32[]{:S(2)}) %all-to-all-start.4) | async-done | bytes 1048608 | tf_op jit(solution)/shard_map/all_to_all | solution.py:148
  668.2 4.1 scatter_custom_fusion.1
  (156 shorter events, 141.0 us)
Async XLA Ops:
  116.8 73.0 %all-gather.4.cloned.1.call-start = ((), (), s32[]{:S(2)}) async-start(), calls=%async_computation.7 | async-start | bytes 2621440 | tf_op jit(solution)/shard_map/all_gather | solution.py:78
  145.5 91.2 %all-gather.6.cloned.1.call-start = ((), (), s32[]{:S(2)}) async-start(), calls=%async_computation.8 | async-start | bytes 2621440 | tf_op jit(solution)/shard_map/all_gather | solution.py:79
  261.7 71.1 %collective-permute-start.3 = (f32[256,1024]{0,1:T(8,128)}, f32[256,1024]{0,1:T(8,128)}, u32[]{:S(2)}, u32[]{:S(2)}) collective-permute-start(f32[256,1024]{0,1:T(8,128)} %bitcast_add_fusion.6), channel_id=1, source_target_pairs={{3,0},{0,1},{1,2},{2,3},{7,4},{4,5},{5,6},{6,7},{11,8},{8,9},{9,10... | collective-permute-start | bytes 3145736 | tf_op jit(solution)/shard_map/while/body/eval_jaxpr/ppermute | solution.py:17
  266.1 66.7 %collective-permute-start.4 = (f32[256,1024]{0,1:T(8,128)}, f32[256,1024]{0,1:T(8,128)}, u32[]{:S(2)}, u32[]{:S(2)}) collective-permute-start(f32[256,1024]{0,1:T(8,128)} %bitcast_add_fusion.7), channel_id=1, source_target_pairs={{3,0},{0,1},{1,2},{2,3},{7,4},{4,5},{5,6},{6,7},{11,8},{8,9},{9,10... | collective-permute-start | bytes 3145736 | tf_op jit(solution)/shard_map/while/body/eval_jaxpr/ppermute | solution.py:17
  267.2 65.6 %collective-permute-start = (bf16[256,1024]{0,1:T(8,128)(2,1)S(1)}, bf16[256,1024]{0,1:T(8,128)(2,1)}, u32[]{:S(2)}, u32[]{:S(2)}) collective-permute-start(bf16[256,1024]{0,1:T(8,128)(2,1)S(1)} %copy.66), channel_id=1, source_target_pairs={{3,0},{0,1},{1,2},{2,3},{7,4},{4,5},{5,6},{6,7},{11,8},{8,9},{9,10... | collective-permute-start | bytes 1572872 | tf_op jit(solution)/shard_map/while/body/eval_jaxpr/ppermute | solution.py:17
  267.8 65.0 %collective-permute-start.1 = (bf16[256,1024]{0,1:T(8,128)(2,1)}, bf16[256,1024]{0,1:T(8,128)(2,1)}, u32[]{:S(2)}, u32[]{:S(2)}) collective-permute-start(bf16[256,1024]{0,1:T(8,128)(2,1)} %copy.67), channel_id=1, source_target_pairs={{3,0},{0,1},{1,2},{2,3},{7,4},{4,5},{5,6},{6,7},{11,8},{8,9},{9,10... | collective-permute-start | bytes 1572872 | tf_op jit(solution)/shard_map/while/body/eval_jaxpr/ppermute | solution.py:17
  270.0 62.8 %collective-permute-start.2 = (s32[256]{0:T(256)S(1)}, s32[256]{0:T(256)S(1)}, u32[]{:S(2)}, u32[]{:S(2)}) collective-permute-start(s32[256]{0:T(256)S(1)} %copy.68), channel_id=1, source_target_pairs={{3,0},{0,1},{1,2},{2,3},{7,4},{4,5},{5,6},{6,7},{11,8},{8,9},{9,10... | collective-permute-start | bytes 3080 | tf_op jit(solution)/shard_map/while/body/eval_jaxpr/ppermute | solution.py:17
  343.1 70.2 %collective-permute-start.3 = (f32[256,1024]{0,1:T(8,128)}, f32[256,1024]{0,1:T(8,128)}, u32[]{:S(2)}, u32[]{:S(2)}) collective-permute-start(f32[256,1024]{0,1:T(8,128)} %bitcast_add_fusion.6), channel_id=1, source_target_pairs={{3,0},{0,1},{1,2},{2,3},{7,4},{4,5},{5,6},{6,7},{11,8},{8,9},{9,10... | collective-permute-start | bytes 3145736 | tf_op jit(solution)/shard_map/while/body/eval_jaxpr/ppermute | solution.py:17
  347.5 65.7 %collective-permute-start.4 = (f32[256,1024]{0,1:T(8,128)}, f32[256,1024]{0,1:T(8,128)}, u32[]{:S(2)}, u32[]{:S(2)}) collective-permute-start(f32[256,1024]{0,1:T(8,128)} %bitcast_add_fusion.7), channel_id=1, source_target_pairs={{3,0},{0,1},{1,2},{2,3},{7,4},{4,5},{5,6},{6,7},{11,8},{8,9},{9,10... | collective-permute-start | bytes 3145736 | tf_op jit(solution)/shard_map/while/body/eval_jaxpr/ppermute | solution.py:17
  347.6 65.7 %collective-permute-start = (bf16[256,1024]{0,1:T(8,128)(2,1)S(1)}, bf16[256,1024]{0,1:T(8,128)(2,1)}, u32[]{:S(2)}, u32[]{:S(2)}) collective-permute-start(bf16[256,1024]{0,1:T(8,128)(2,1)S(1)} %copy.66), channel_id=1, source_target_pairs={{3,0},{0,1},{1,2},{2,3},{7,4},{4,5},{5,6},{6,7},{11,8},{8,9},{9,10... | collective-permute-start | bytes 1572872 | tf_op jit(solution)/shard_map/while/body/eval_jaxpr/ppermute | solution.py:17
  347.7 65.6 %collective-permute-start.1 = (bf16[256,1024]{0,1:T(8,128)(2,1)}, bf16[256,1024]{0,1:T(8,128)(2,1)}, u32[]{:S(2)}, u32[]{:S(2)}) collective-permute-start(bf16[256,1024]{0,1:T(8,128)(2,1)} %copy.67), channel_id=1, source_target_pairs={{3,0},{0,1},{1,2},{2,3},{7,4},{4,5},{5,6},{6,7},{11,8},{8,9},{9,10... | collective-permute-start | bytes 1572872 | tf_op jit(solution)/shard_map/while/body/eval_jaxpr/ppermute | solution.py:17
  351.4 61.9 %collective-permute-start.2 = (s32[256]{0:T(256)S(1)}, s32[256]{0:T(256)S(1)}, u32[]{:S(2)}, u32[]{:S(2)}) collective-permute-start(s32[256]{0:T(256)S(1)} %copy.68), channel_id=1, source_target_pairs={{3,0},{0,1},{1,2},{2,3},{7,4},{4,5},{5,6},{6,7},{11,8},{8,9},{9,10... | collective-permute-start | bytes 3080 | tf_op jit(solution)/shard_map/while/body/eval_jaxpr/ppermute | solution.py:17
  423.6 69.3 %collective-permute-start.3 = (f32[256,1024]{0,1:T(8,128)}, f32[256,1024]{0,1:T(8,128)}, u32[]{:S(2)}, u32[]{:S(2)}) collective-permute-start(f32[256,1024]{0,1:T(8,128)} %bitcast_add_fusion.6), channel_id=1, source_target_pairs={{3,0},{0,1},{1,2},{2,3},{7,4},{4,5},{5,6},{6,7},{11,8},{8,9},{9,10... | collective-permute-start | bytes 3145736 | tf_op jit(solution)/shard_map/while/body/eval_jaxpr/ppermute | solution.py:17
  428.1 64.8 %collective-permute-start.4 = (f32[256,1024]{0,1:T(8,128)}, f32[256,1024]{0,1:T(8,128)}, u32[]{:S(2)}, u32[]{:S(2)}) collective-permute-start(f32[256,1024]{0,1:T(8,128)} %bitcast_add_fusion.7), channel_id=1, source_target_pairs={{3,0},{0,1},{1,2},{2,3},{7,4},{4,5},{5,6},{6,7},{11,8},{8,9},{9,10... | collective-permute-start | bytes 3145736 | tf_op jit(solution)/shard_map/while/body/eval_jaxpr/ppermute | solution.py:17
  428.1 64.8 %collective-permute-start = (bf16[256,1024]{0,1:T(8,128)(2,1)S(1)}, bf16[256,1024]{0,1:T(8,128)(2,1)}, u32[]{:S(2)}, u32[]{:S(2)}) collective-permute-start(bf16[256,1024]{0,1:T(8,128)(2,1)S(1)} %copy.66), channel_id=1, source_target_pairs={{3,0},{0,1},{1,2},{2,3},{7,4},{4,5},{5,6},{6,7},{11,8},{8,9},{9,10... | collective-permute-start | bytes 1572872 | tf_op jit(solution)/shard_map/while/body/eval_jaxpr/ppermute | solution.py:17
  428.1 64.8 %collective-permute-start.1 = (bf16[256,1024]{0,1:T(8,128)(2,1)}, bf16[256,1024]{0,1:T(8,128)(2,1)}, u32[]{:S(2)}, u32[]{:S(2)}) collective-permute-start(bf16[256,1024]{0,1:T(8,128)(2,1)} %copy.67), channel_id=1, source_target_pairs={{3,0},{0,1},{1,2},{2,3},{7,4},{4,5},{5,6},{6,7},{11,8},{8,9},{9,10... | collective-permute-start | bytes 1572872 | tf_op jit(solution)/shard_map/while/body/eval_jaxpr/ppermute | solution.py:17
  431.9 61.0 %collective-permute-start.2 = (s32[256]{0:T(256)S(1)}, s32[256]{0:T(256)S(1)}, u32[]{:S(2)}, u32[]{:S(2)}) collective-permute-start(s32[256]{0:T(256)S(1)} %copy.68), channel_id=1, source_target_pairs={{3,0},{0,1},{1,2},{2,3},{7,4},{4,5},{5,6},{6,7},{11,8},{8,9},{9,10... | collective-permute-start | bytes 3080 | tf_op jit(solution)/shard_map/while/body/eval_jaxpr/ppermute | solution.py:17
  503.2 68.4 %collective-permute-start.3 = (f32[256,1024]{0,1:T(8,128)}, f32[256,1024]{0,1:T(8,128)}, u32[]{:S(2)}, u32[]{:S(2)}) collective-permute-start(f32[256,1024]{0,1:T(8,128)} %bitcast_add_fusion.6), channel_id=1, source_target_pairs={{3,0},{0,1},{1,2},{2,3},{7,4},{4,5},{5,6},{6,7},{11,8},{8,9},{9,10... | collective-permute-start | bytes 3145736 | tf_op jit(solution)/shard_map/while/body/eval_jaxpr/ppermute | solution.py:17
  507.6 63.9 %collective-permute-start.4 = (f32[256,1024]{0,1:T(8,128)}, f32[256,1024]{0,1:T(8,128)}, u32[]{:S(2)}, u32[]{:S(2)}) collective-permute-start(f32[256,1024]{0,1:T(8,128)} %bitcast_add_fusion.7), channel_id=1, source_target_pairs={{3,0},{0,1},{1,2},{2,3},{7,4},{4,5},{5,6},{6,7},{11,8},{8,9},{9,10... | collective-permute-start | bytes 3145736 | tf_op jit(solution)/shard_map/while/body/eval_jaxpr/ppermute | solution.py:17
  507.6 63.9 %collective-permute-start = (bf16[256,1024]{0,1:T(8,128)(2,1)S(1)}, bf16[256,1024]{0,1:T(8,128)(2,1)}, u32[]{:S(2)}, u32[]{:S(2)}) collective-permute-start(bf16[256,1024]{0,1:T(8,128)(2,1)S(1)} %copy.66), channel_id=1, source_target_pairs={{3,0},{0,1},{1,2},{2,3},{7,4},{4,5},{5,6},{6,7},{11,8},{8,9},{9,10... | collective-permute-start | bytes 1572872 | tf_op jit(solution)/shard_map/while/body/eval_jaxpr/ppermute | solution.py:17
  507.6 63.9 %collective-permute-start.1 = (bf16[256,1024]{0,1:T(8,128)(2,1)}, bf16[256,1024]{0,1:T(8,128)(2,1)}, u32[]{:S(2)}, u32[]{:S(2)}) collective-permute-start(bf16[256,1024]{0,1:T(8,128)(2,1)} %copy.67), channel_id=1, source_target_pairs={{3,0},{0,1},{1,2},{2,3},{7,4},{4,5},{5,6},{6,7},{11,8},{8,9},{9,10... | collective-permute-start | bytes 1572872 | tf_op jit(solution)/shard_map/while/body/eval_jaxpr/ppermute | solution.py:17
  511.5 60.1 %collective-permute-start.2 = (s32[256]{0:T(256)S(1)}, s32[256]{0:T(256)S(1)}, u32[]{:S(2)}, u32[]{:S(2)}) collective-permute-start(s32[256]{0:T(256)S(1)} %copy.68), channel_id=1, source_target_pairs={{3,0},{0,1},{1,2},{2,3},{7,4},{4,5},{5,6},{6,7},{11,8},{8,9},{9,10... | collective-permute-start | bytes 3080 | tf_op jit(solution)/shard_map/while/body/eval_jaxpr/ppermute | solution.py:17
  576.0 33.1 %all-to-all-start.5 = ((bf16[32,16,1024]{2,1,0:T(8,128)(2,1)}), bf16[32,16,1024]{2,1,0:T(8,128)(2,1)S(1)}, u32[]{:S(2)}, u32[]{:S(2)}) async-start(bf16[32,16,1024]{2,1,0:T(8,128)(2,1)} %bitcast.20), calls=%async_computation.5 | async-start | bytes 2097152 | tf_op jit(solution)/shard_map/all_to_all | solution.py:151
  638.6 29.6 %all-to-all-start.4 = ((bf16[32,16,1024]{2,1,0:T(8,128)(2,1)}), bf16[32,16,1024]{2,1,0:T(8,128)(2,1)}, u32[]{:S(2)}, u32[]{:S(2)}) async-start(bf16[32,16,1024]{2,1,0:T(8,128)(2,1)} %bitcast.18), calls=%async_computation.4 | async-start | bytes 2097152 | tf_op jit(solution)/shard_map/all_to_all | solution.py:148
  (12 other events, 308.3 us)
Sparse Core Ops, SparseCore 0:
  145.7 44.0 all-gather.3
  191.9 44.7 all-gather.5
where the time goes:
time: 681 us; the launch traced here: 679 us
  waiting for transfers between devices  380 us (56%)
  blocking collectives  98.3 us (14%)
  local copies, waits for them, and re-layouts  69.5 us (10%)
  other arithmetic  43.5 us (6%)
  matrix products  41.3 us (6%)
  starting transfers between devices  31.9 us (5%)
  between operations  15 us (2%)
    ppermute x20, waiting for transfers between devices, shifted(): return lax.ppermute(block, axis, route)  234 us
    all_to_all x1, blocking collectives, shards(): lax.all_to_all(pack_rows(values), ('group', 'blk'), split_axis=0, concat_...  33.2 us
    all_gather x1, waiting for transfers between devices, shards(): key_piece = lax.all_gather(key_rows, 'blk', axis=0, tiled=True)  31.2 us
    all_gather x1, waiting for transfers between devices, shards(): value_piece = lax.all_gather(value_rows, 'blk', axis=0, tiled=True)  31 us
    all_to_all x1, blocking collectives, shards(): lax.all_to_all(pack_rows(out_grad), ('group', 'blk'), split_axis=0, conca...  29.4 us
    all_to_all x1, blocking collectives, shards(): lax.all_to_all(pack_rows(queries), ('group', 'blk'), split_axis=0, concat...  29.4 us
    all_to_all x1, waiting for transfers between devices, shards(): lax.all_to_all(unpack_rows(key_grad), ('group', 'blk'), split_axis=0, con...  22.2 us
    all_to_all x1, waiting for transfers between devices, shards(): lax.all_to_all(unpack_rows(value_grad), ('group', 'blk'), split_axis=0, c...  20.8 us
  transfers between devices with their start and end apart: 26, of which 10 were waited for; matrix products, arithmetic and copies ran while one was open for 10% of the time, Pallas kernels for 0%

commit v1 on v0

v1 whole, which is shorter than its diff:
```python
import functools

import jax
import jax.numpy as jnp
from jax import lax
from jax.experimental import pallas as pl
from jax.experimental.pallas import tpu as pltpu
from jax.sharding import PartitionSpec as P

HEAD_DIM = 64
PAIR = 2 * HEAD_DIM
MESH = pl.DeviceIdType.MESH
VMEM_LIMIT = 56 * 1024 * 1024


def turned(index, by, size):
    return lax.rem(index + by, size)


def greet(n_g, n_b, g, z):
    barrier = pltpu.get_barrier_semaphore()
    for i in range(1, n_b):
        pl.semaphore_signal(barrier, inc=1, device_id=(g, turned(z, i, n_b)), device_id_type=MESH)
    for i in range(1, n_g):
        pl.semaphore_signal(barrier, inc=1, device_id=(turned(g, i, n_g), z), device_id_type=MESH)
    pl.semaphore_wait(barrier, n_b + n_g - 2)


def remote(src, dst, send_sem, recv_sem, device):
    return pltpu.make_async_remote_copy(
        src_ref=src,
        dst_ref=dst,
        send_sem=send_sem,
        recv_sem=recv_sem,
        device_id=device,
        device_id_type=MESH,
    )


def send_hot(plan, rows, slots):
    named = plan[0:1, :slots]
    at = lax.broadcasted_iota(jnp.int32, (rows, slots), 0)
    return jnp.where(at == named, 1.0, 0.0).astype(jnp.float32)


def take_hot(plan, rows, dims, b):
    n_g, n_b, cap = dims
    taken = plan[1:2, :rows]
    if cap % 16 == 0:
        slot = lax.broadcasted_iota(jnp.int32, (n_g * n_b * cap, rows), 0)
    else:
        place = lax.broadcasted_iota(jnp.int32, (n_g * n_b * n_b * cap, rows), 0)
        slot = place // (n_b * cap) * cap + place % cap
        slot = jnp.where(place // cap % n_b == b, slot, -1)
    return jnp.where(slot == taken, 1.0, 0.0).astype(jnp.float32)


def regroup_kernel(
    dims, plan_ref, q, k, v, d, out_q, out_k, out_v, out_d, out_plan,
    plans, zbuf, sbuf, rbuf, pmat, umat,
    plan_s, plan_r, zs, zr, zl, gs, gr,
):
    n_g, n_b, cap = dims
    g, z = lax.axis_index("group"), lax.axis_index("blk")
    rows, width = zbuf.shape[2], zbuf.shape[3]
    slots = n_g * n_b * cap
    arrays = (q, k, v, d)
    outs = (out_q, out_k, out_v, out_d)
    greet(n_g, n_b, g, z)

    plan_sends = []
    for i in range(1, n_b):
        to = turned(z, i, n_b)
        copy = remote(plan_ref, plans.at[z], plan_s.at[to], plan_r.at[z], (g, to))
        copy.start()
        plan_sends.append(copy)

    def columns(index):
        return pl.ds(pl.multiple_of(index * width, width), width)

    z_sends, z_locals = [], []
    for a, array in enumerate(arrays):
        for i in range(1, n_b):
            to = turned(z, i, n_b)
            copy = remote(array.at[:, columns(to)], zbuf.at[a, z], zs.at[a, to], zr.at[a, z], (g, to))
            copy.start()
            z_sends.append(copy)
        local = pltpu.make_async_copy(array.at[:, columns(z)], zbuf.at[a, z], zl.at[a])
        local.start()
        z_locals.append(local)

    plans[z] = plan_ref[...]
    for i in range(1, n_b):
        source = turned(z, i, n_b)
        remote(plan_ref, plans.at[source], plan_s.at[source], plan_r.at[source], (g, source)).wait_recv()
    for b in range(n_b):
        plan = plans[b]
        out_plan[b] = plan
        pmat[b] = send_hot(plan, rows, slots).T.astype(jnp.bfloat16)
        umat[b] = take_hot(plan, rows, dims, b).T.astype(jnp.bfloat16)

    g_sends = []
    for a, array in enumerate(arrays):
        z_locals[a].wait()
        for i in range(1, n_b):
            source = turned(z, i, n_b)
            remote(
                array.at[:, columns(source)], zbuf.at[a, source], zs.at[a, source], zr.at[a, source], (g, source)
            ).wait_recv()
        for b in range(n_b):
            packed = jnp.dot(pmat[b], zbuf[a, b], preferred_element_type=jnp.float32)
            sbuf[a, :, b] = packed.astype(jnp.bfloat16).reshape(n_g, n_b * cap, width)
        for i in range(1, n_g):
            to = turned(g, i, n_g)
            copy = remote(sbuf.at[a, to], rbuf.at[a, g], gs.at[a, to], gr.at[a, g], (to, z))
            copy.start()
            g_sends.append(copy)
        rbuf[a, g] = sbuf[a, g]

    for a in range(len(arrays)):
        for i in range(1, n_g):
            source = turned(g, i, n_g)
            remote(
                sbuf.at[a, source], rbuf.at[a, source], gs.at[a, source], gr.at[a, source], (source, z)
            ).wait_recv()
        for b in range(n_b):
            if cap % 16 == 0:
                held = rbuf[a, :, :, b * cap : (b + 1) * cap]
            else:
                held = rbuf[a]
            held = held.reshape(-1, width)
            placed = jnp.dot(umat[b], held, preferred_element_type=jnp.float32)
            outs[a][b * rows : (b + 1) * rows, :] = placed.astype(jnp.bfloat16)

    for copy in plan_sends + z_sends + g_sends:
        copy.wait_send()


def restore_kernel(
    dims, plans, dq, dk, dv, out_q, out_k, out_v,
    sbuf, rbuf, zbuf, pmat, umat, gs, gr, zs, zr, zl,
):
    n_g, n_b, cap = dims
    g, z = lax.axis_index("group"), lax.axis_index("blk")
    rows, width = zbuf.shape[2], zbuf.shape[3]
    slots = n_g * n_b * cap
    arrays = (dq, dk, dv)
    outs = (out_q, out_k, out_v)
    greet(n_g, n_b, g, z)

    def columns(index):
        return pl.ds(pl.multiple_of(index * width, width), width)

    for b in range(n_b):
        umat[b] = take_hot(plans[b], rows, dims, b).astype(jnp.bfloat16)

    g_sends = []
    for a, array in enumerate(arrays):
        if cap % 16 == 0:
            for b in range(n_b):
                packed = jnp.dot(
                    umat[b], array[b * rows : (b + 1) * rows, :], preferred_element_type=jnp.float32
                )
                sbuf[a, :, :, b * cap : (b + 1) * cap] = packed.astype(jnp.bfloat16).reshape(
                    n_g, n_b, cap, width
                )
        else:
            packed = jnp.zeros((slots * n_b, width), jnp.float32)
            for b in range(n_b):
                packed += jnp.dot(
                    umat[b], array[b * rows : (b + 1) * rows, :], preferred_element_type=jnp.float32
                )
            sbuf[a] = packed.astype(jnp.bfloat16).reshape(n_g, n_b, n_b * cap, width)
        for i in range(1, n_g):
            to = turned(g, i, n_g)
            copy = remote(sbuf.at[a, to], rbuf.at[a, g], gs.at[a, to], gr.at[a, g], (to, z))
            copy.start()
            g_sends.append(copy)
        rbuf[a, g] = sbuf[a, g]

    for b in range(n_b):
        pmat[b] = send_hot(plans[b], rows, slots).astype(jnp.bfloat16)

    z_sends, z_locals = [], []
    for a in range(len(arrays)):
        for i in range(1, n_g):
            source = turned(g, i, n_g)
            remote(
                sbuf.at[a, source], rbuf.at[a, source], gs.at[a, source], gr.at[a, source], (source, z)
            ).wait_recv()
        for b in range(n_b):
            held = rbuf[a, :, b].reshape(slots, width)
            placed = jnp.dot(pmat[b], held, preferred_element_type=jnp.float32)
            zbuf[a, b] = placed.astype(jnp.bfloat16)
        for i in range(1, n_b):
            to = turned(z, i, n_b)
            copy = remote(zbuf.at[a, to], outs[a].at[:, columns(z)], zs.at[a, to], zr.at[a, z], (g, to))
            copy.start()
            z_sends.append(copy)
        local = pltpu.make_async_copy(zbuf.at[a, z], outs[a].at[:, columns(z)], zl.at[a])
        local.start()
        z_locals.append(local)

    for a in range(len(arrays)):
        z_locals[a].wait()
        for i in range(1, n_b):
            source = turned(z, i, n_b)
            remote(
                zbuf.at[a, source], outs[a].at[:, columns(source)], zs.at[a, source], zr.at[a, source], (g, source)
            ).wait_recv()
    for copy in g_sends + z_sends:
        copy.wait_send()


def dot_last(left, right):
    return lax.dot_general(left, right, (((1,), (1,)), ((), ())), preferred_element_type=jnp.float32)


def attend_kernel(n_b, scenes, q, k, v, d, dq, dk, dv, acc_k, acc_v):
    rows = q.shape[0] // n_b
    scale = HEAD_DIM ** (-0.5)
    acc_k[...] = jnp.zeros_like(acc_k)
    acc_v[...] = jnp.zeros_like(acc_v)
    lane = lax.broadcasted_iota(jnp.int32, (1, PAIR), 1)

    def of_head(array, head):
        inside = (lane >= head * HEAD_DIM) & (lane < (head + 1) * HEAD_DIM)
        return jnp.where(inside, array, jnp.zeros_like(array))

    def frame(i, first, count):
        at = pl.ds(pl.multiple_of(i * rows, rows), rows)
        near = pl.ds(pl.multiple_of(first * rows, rows), count * rows)
        q_rows, d_rows = q[at, :], d[at, :]
        k_rows, v_rows = k[near, :], v[near, :]
        k_turned = k_rows.T
        q_scaled = (q_rows.astype(jnp.float32) * scale).astype(jnp.bfloat16)
        turned_grads, add_k, add_v = [], None, None
        for head in range(2):
            d_head = of_head(d_rows, head)
            scores = dot_last(k_rows, of_head(q_scaled, head))
            weight_grad = dot_last(v_rows, d_head)
            weights = jnp.exp(scores - jnp.max(scores, axis=0, keepdims=True))
            inverse = 1.0 / jnp.sum(weights, axis=0, keepdims=True)
            weights = weights * inverse
            row_dot = jnp.sum(weights * weight_grad, axis=0, keepdims=True)
            score_half = (weights * (weight_grad - row_dot) * scale).astype(jnp.bfloat16)
            weight_half = weights.astype(jnp.bfloat16)
            turned_grads.append(
                jnp.dot(
                    k_turned[head * HEAD_DIM : (head + 1) * HEAD_DIM, :],
                    score_half,
                    preferred_element_type=jnp.float32,
                )
            )
            part_k = jnp.dot(score_half, of_head(q_rows, head), preferred_element_type=jnp.float32)
            part_v = jnp.dot(weight_half, d_head, preferred_element_type=jnp.float32)
            add_k = part_k if add_k is None else add_k + part_k
            add_v = part_v if add_v is None else add_v + part_v
        dq[at, :] = jnp.concatenate(turned_grads, axis=0).T.astype(jnp.bfloat16)
        acc_k[near, :] += add_k
        acc_v[near, :] += add_v

    def step(i, carry):
        mine = scenes[i]
        first, count = jnp.int32(0), jnp.int32(0)
        for j in range(n_b):
            first += jnp.where(scenes[j] < mine, 1, 0)
            count += jnp.where(scenes[j] == mine, 1, 0)
        for n in range(1, n_b):
            pl.when(count == n)(functools.partial(frame, i, first, n))
        return carry

    lax.fori_loop(0, n_b, step, 0)
    dk[...] = acc_k[...].astype(jnp.bfloat16)
    dv[...] = acc_v[...].astype(jnp.bfloat16)


def shards(n_g, n_b, queries, keys, values, out_grad, send_rows, recv_slots, scene_frames):
    rows, features = queries.shape
    cap = send_rows.shape[2]
    dims = (n_g, n_b, cap)
    slots = n_g * n_b * cap
    width = features // n_b
    long = max(slots, rows)
    plan = jnp.concatenate(
        [
            jnp.pad(send_rows.reshape(1, slots), ((0, 0), (0, long - slots))),
            jnp.pad(recv_slots, ((0, 0), (0, long - rows))),
            jnp.broadcast_to(scene_frames, (6, long)),
        ],
        axis=0,
    )
    in_vmem = pl.BlockSpec(memory_space=pltpu.VMEM)
    anywhere = pl.BlockSpec(memory_space=pl.ANY)
    group_rows = n_b * rows
    taken = slots if cap % 16 == 0 else slots * n_b
    half = jnp.bfloat16
    dma = pltpu.SemaphoreType.DMA
    *inbound, plans = pl.pallas_call(
        functools.partial(regroup_kernel, dims),
        out_shape=[jax.ShapeDtypeStruct((group_rows, width), half)] * 4
        + [jax.ShapeDtypeStruct((n_b, 8, long), jnp.int32)],
        in_specs=[in_vmem] + [anywhere] * 4,
        out_specs=[in_vmem] * 5,
        scratch_shapes=[
            pltpu.VMEM((n_b, 8, long), jnp.int32),
            pltpu.VMEM((4, n_b, rows, width), half),
            pltpu.VMEM((4, n_g, n_b, n_b * cap, width), half),
            pltpu.VMEM((4, n_g, n_b, n_b * cap, width), half),
            pltpu.VMEM((n_b, slots, rows), half),
            pltpu.VMEM((n_b, rows, taken), half),
            dma((n_b,)),
            dma((n_b,)),
            dma((4, n_b)),
            dma((4, n_b)),
            dma((4,)),
            dma((4, n_g)),
            dma((4, n_g)),
        ],
        compiler_params=pltpu.CompilerParams(
            collective_id=0, has_side_effects=True, vmem_limit_bytes=VMEM_LIMIT
        ),
        name="regroup",
    )(plan, queries, keys, values, out_grad)

    pair = pl.BlockSpec((group_rows, PAIR), lambda i, scenes: (0, i))
    grads = pl.pallas_call(
        functools.partial(attend_kernel, n_b),
        out_shape=[jax.ShapeDtypeStruct((group_rows, width), half)] * 3,
        grid_spec=pltpu.PrefetchScalarGridSpec(
            num_scalar_prefetch=1,
            grid=(width // PAIR,),
            in_specs=[pair] * 4,
            out_specs=[pair] * 3,
            scratch_shapes=[pltpu.VMEM((group_rows, PAIR), jnp.float32)] * 2,
        ),
        compiler_params=pltpu.CompilerParams(vmem_limit_bytes=VMEM_LIMIT),
        name="attend",
    )(plans[:, 2, 0], *inbound)

    return tuple(
        pl.pallas_call(
            functools.partial(restore_kernel, dims),
            out_shape=[jax.ShapeDtypeStruct((rows, features), half)] * 3,
            in_specs=[in_vmem] * 4,
            out_specs=[anywhere] * 3,
            scratch_shapes=[
                pltpu.VMEM((3, n_g, n_b, n_b * cap, width), half),
                pltpu.VMEM((3, n_g, n_b, n_b * cap, width), half),
                pltpu.VMEM((3, n_b, rows, width), half),
                pltpu.VMEM((n_b, rows, slots), half),
                pltpu.VMEM((n_b, taken, rows), half),
                dma((3, n_g)),
                dma((3, n_g)),
                dma((3, n_b)),
                dma((3, n_b)),
                dma((3,)),
            ],
            compiler_params=pltpu.CompilerParams(
                collective_id=1, has_side_effects=True, vmem_limit_bytes=VMEM_LIMIT
            ),
            name="restore",
        )(plans, *grads)
    )


def solution(mesh):
    both = P(("group", "blk"), None)
    placed = (both, both, both, both, P(("group", "blk"), None, None), both, P("group", "blk"))
    return jax.shard_map(
        functools.partial(shards, mesh.shape["group"], mesh.shape["blk"]),
        mesh=mesh,
        in_specs=placed,
        out_specs=(both, both, both),
        check_vma=False,
    )
```

time: 681 us -> 157 us (0.23)
  waiting for transfers between devices: 380 us -> 0 us
  Pallas kernels: 0 us -> 146 us
  blocking collectives: 98.3 us -> 0 us
  local copies, waits for them, and re-layouts: 69.5 us -> 6.94 us
  other arithmetic: 43.5 us -> 0.67 us
  matrix products: 41.3 us -> 0 us
  starting transfers between devices: 31.9 us -> 0 us
  between operations: 15 us -> 1.31 us
    ppermute x20 -> x0, waiting for transfers between devices: 234 us -> none  [shifted(): return lax.ppermute(block, axis, route)]
    pallas_call x0 -> x3, Pallas kernels: none -> 146 us  [the longest x1 72.4 us: shards(): pl.pallas_call(functools.partial(regroup_kernel, dims), out_shape=[jax.Sh...]
    all_to_all x3 -> x0, blocking collectives: 92.1 us -> none  [the longest x1 33.2 us: shards(): lax.all_to_all(pack_rows(values), ('group', 'blk'), split_axis=0, concat_...]
    all_to_all x4 -> x0, waiting for transfers between devices: 82.4 us -> none  [the longest x1 22.2 us: shards(): lax.all_to_all(unpack_rows(key_grad), ('group', 'blk'), split_axis=0, con...]
    all_gather x2 -> x0, waiting for transfers between devices: 62.2 us -> none  [the longest x1 31.2 us: shards(): key_piece = lax.all_gather(key_rows, 'blk', axis=0, tiled=True)]
    dot_general x22 -> x0, matrix products: 41.3 us -> none  [the longest x4 12.7 us: block_terms(): jnp.einsum('qhd,khd->hqk', grad_heads, value_heads, preferred_element_typ...]
    add x12 -> x0, other arithmetic: 26.9 us -> none  [the longest x4 9.24 us: cycle_block(): accums[1]]
    scatter x6 -> x0, local copies, waits for them, and re-layouts: 19.8 us -> none  [the longest x3 11 us: restore_rows(): return jnp.zeros((row_count, feature_width), jnp.bfloat16).at[send_plan.r...]
  transfers between devices with their start and end apart: 26 -> 0, of which waited for: 10 -> 0; matrix products, arithmetic and copies ran while one was open for 10% -> 0% of each run, Pallas kernels for 0% -> 0%
where the time goes in v1:
time: 157 us; the launch traced here: 155 us
  Pallas kernels  146 us (93%)
  local copies, waits for them, and re-layouts  6.94 us (4%)
    pallas_call x1, Pallas kernels, shards(): pl.pallas_call(functools.partial(regroup_kernel, dims), out_shape=[jax.Sh...  72.4 us
    pallas_call x1, Pallas kernels, shards(): pl.pallas_call(functools.partial(restore_kernel, dims), out_shape=[jax.Sh...  59.2 us
    pallas_call x1, Pallas kernels, shards(): pl.pallas_call(functools.partial(attend_kernel, n_b), out_shape=[jax.Shap...  14.8 us
    unnamed x10, local copies, waits for them, and re-layouts  5.32 us

profile of v1, /device:TPU:1, one launch (start us, length us, event | category | flops | bytes accessed | tf_op | source)
XLA Modules:
  0.0 155.3 jit_solution(6649771984996362764)
XLA Ops:
  1.3 0.1 pad.7.clone
  1.4 0.8 copy.11
  2.1 0.0 copy-start.2
  2.1 0.1 reshape.9
  2.2 0.6 copy-done.2
  2.8 0.7 fusion.plan_ref
  3.5 72.4 %regroup.1 = (bf16[1024,256]{1,0:T(8,128)(2,1)}, bf16[1024,256]{1,0:T(8,128)(2,1)}, bf16[1024,256]{1,0:T(8,128)(2,1)}, bf16[1024,256]{1,0:T(8,128)(2,1)}, s32[4,8,512]{2,1,0:T(8,128)}) custom-call(s32[8,512]{1,0:T(8,128)} %fusion.plan_ref, bf16[256,1024]{1,0:T(8,128)(2,1)} %q.1, bf16[256,1024]{1,0:T(8,128)(2,1)} %k.1, bf16[256,1024]{1,0:T(8,128)(2,1)} %v.1, ...), custom_call_target="tpu_custom_call" | custom-call | tf_op jit(solution)/shard_map/regroup/pallas_call | solution.py:299
  75.9 1.5 slice_reduce_fusion.scenes
  77.3 14.8 %attend.1 = (bf16[1024,256]{1,0:T(8,128)(2,1)}, bf16[1024,256]{1,0:T(8,128)(2,1)}, bf16[1024,256]{1,0:T(8,128)(2,1)}) custom-call(s32[4]{0:T(128)} %slice_reduce_fusion.scenes, bf16[1024,256]{1,0:T(8,128)(2,1)} %get-tuple-element.12.q, bf16[1024,256]{1,0:T(8,128)(2,1)} %get-tuple-element.13.k, bf16[1024,256]{1,0:T(8,128)(2,1)} %get-tuple-element.14.v, ...), custom_call_target="tpu_custom_call" | custom-call | tf_op jit(solution)/shard_map/attend/pallas_call | solution.py:327
  92.2 59.2 %restore.1 = (bf16[256,1024]{1,0:T(8,128)(2,1)}, bf16[256,1024]{1,0:T(8,128)(2,1)}, bf16[256,1024]{1,0:T(8,128)(2,1)}) custom-call(s32[4,8,512]{2,1,0:T(8,128)} %get-tuple-element.11.plans, bf16[1024,256]{1,0:T(8,128)(2,1)} %get-tuple-element.16.dq, bf16[1024,256]{1,0:T(8,128)(2,1)} %get-tuple-element.17.dk, bf16[1024,256]{1,0:T(8,128)(2,1)} %get-tuple-element.18.dv), custom_call_target="tpu_custom_call" | custom-call | tf_op jit(solution)/shard_map/restore/pallas_call | solution.py:342
  151.4 0.0 copy-start.1
  151.4 1.9 %copy.16 = bf16[256,1024]{1,0:T(8,128)(2,1)} copy(bf16[256,1024]{1,0:T(8,128)(2,1)} %get-tuple-element.22) | data formatting | bytes 1048576
  153.3 0.0 copy-done.1
  153.3 0.0 copy-start
  153.3 0.8 copy.17
  154.1 0.4 copy-done
  154.6 0.8 copy.18
  (1 shorter events, 0.0 us)
Async XLA Ops:
  2.1 0.7 copy-start.2
  151.4 1.9 %copy-start.1 = (bf16[256,1024]{1,0:T(8,128)(2,1)S(1)}, bf16[256,1024]{1,0:T(8,128)(2,1)}, u32[]{:S(2)}) copy-start(bf16[256,1024]{1,0:T(8,128)(2,1)} %get-tuple-element.23) | copy-start | bytes 1572868
  153.3 1.2 copy-start

commit v2 on v0

v2 whole, which is shorter than its diff:
```python
import functools

import jax
import jax.numpy as jnp
from jax import lax
from jax.experimental import pallas as pl
from jax.experimental.pallas import tpu as pltpu
from jax.sharding import PartitionSpec as P

HEAD_DIM = 64
PAIR = 2 * HEAD_DIM
MESH = pl.DeviceIdType.MESH
LOW_SCORE = -1e30
DEPTH = 3
VMEM_LIMIT = 56 * 1024 * 1024


def turned(index, by, size):
    return lax.rem(index + by, size)


def greet(n_g, n_b, g, z):
    barrier = pltpu.get_barrier_semaphore()
    for i in range(1, n_b):
        pl.semaphore_signal(barrier, inc=1, device_id=(g, turned(z, i, n_b)), device_id_type=MESH)
    for i in range(1, n_g):
        pl.semaphore_signal(barrier, inc=1, device_id=(turned(g, i, n_g), z), device_id_type=MESH)
    pl.semaphore_wait(barrier, n_b + n_g - 2)


def remote(src, dst, send_sem, recv_sem, device):
    return pltpu.make_async_remote_copy(
        src_ref=src,
        dst_ref=dst,
        send_sem=send_sem,
        recv_sem=recv_sem,
        device_id=device,
        device_id_type=MESH,
    )


def send_hot(plan, rows, slots):
    named = plan[0:1, :slots]
    at = lax.broadcasted_iota(jnp.int32, (rows, slots), 0)
    return jnp.where(at == named, 1.0, 0.0).astype(jnp.float32)


def take_hot(plan, rows, dims, b):
    n_g, n_b, cap = dims
    taken = plan[1:2, :rows]
    if cap % 16 == 0:
        slot = lax.broadcasted_iota(jnp.int32, (n_g * n_b * cap, rows), 0)
    else:
        place = lax.broadcasted_iota(jnp.int32, (n_g * n_b * n_b * cap, rows), 0)
        slot = place // (n_b * cap) * cap + place % cap
        slot = jnp.where(place // cap % n_b == b, slot, -1)
    return jnp.where(slot == taken, 1.0, 0.0).astype(jnp.float32)


def dot_first(left, right):
    return lax.dot_general(left, right, (((0,), (0,)), ((), ())), preferred_element_type=jnp.float32)


def dot_last(left, right):
    return lax.dot_general(left, right, (((1,), (1,)), ((), ())), preferred_element_type=jnp.float32)


def fused_kernel(
    dims, plan_ref, q, k, v, d, out_q, out_k, out_v,
    plans, zbuf, sbuf, rbuf, held, grads, back_s, back_r, back_z, acc_k, acc_v, pack, unpack, pack_t, unpack_t,
    plan_s, plan_r, zs, zr, zl, gs, gr, bgs, bgr, bzs, bzr, bzl,
):
    n_g, n_b, cap = dims
    g, z = lax.axis_index("group"), lax.axis_index("blk")
    rows = zbuf.shape[2]
    features = q.shape[1]
    width = features // n_b
    chunks = width // PAIR
    slots = n_g * n_b * cap
    aligned = cap % 16 == 0
    arrays = (q, k, v, d)
    outs = (out_q, out_k, out_v)
    steps = 4 * chunks
    scale = HEAD_DIM ** (-0.5)
    half = jnp.bfloat16
    z_others = [turned(z, i, n_b) for i in range(1, n_b)]
    g_others = [turned(g, i, n_g) for i in range(1, n_g)]
    sends = []

    def columns(index, chunk):
        return pl.ds(pl.multiple_of(index * width + chunk * PAIR, PAIR), PAIR)

    def go(copy):
        copy.start()
        sends.append(copy)

    def start_z(t):
        chunk, a = divmod(t, 4)
        for to in z_others:
            go(remote(arrays[a].at[:, columns(to, chunk)], zbuf.at[t, z], zs.at[t, to], zr.at[t, z], (g, to)))
        pltpu.make_async_copy(arrays[a].at[:, columns(z, chunk)], zbuf.at[t, z], zl.at[t]).start()

    def pack_step(t):
        chunk, a = divmod(t, 4)
        pltpu.make_async_copy(arrays[a].at[:, columns(z, chunk)], zbuf.at[t, z], zl.at[t]).wait()
        for other in z_others:
            remote(
                arrays[a].at[:, columns(other, chunk)],
                zbuf.at[t, other], zs.at[t, other], zr.at[t, other], (g, other),
            ).wait_recv()
        for b in range(n_b):
            packed = jnp.dot(pack[b], zbuf[t, b], preferred_element_type=jnp.float32)
            sbuf[t, :, b] = packed.astype(half).reshape(n_g, n_b * cap, PAIR)
        for to in g_others:
            go(remote(sbuf.at[t, to], rbuf.at[t, g], gs.at[t, to], gr.at[t, g], (to, z)))
        rbuf[t, g] = sbuf[t, g]

    def unpack_step(t):
        for other in g_others:
            remote(sbuf.at[t, other], rbuf.at[t, other], gs.at[t, other], gr.at[t, other], (other, z)).wait_recv()
        for b in range(n_b):
            if aligned:
                came = rbuf[t, :, :, b * cap : (b + 1) * cap].reshape(slots, PAIR)
                placed = jnp.dot(unpack[b], came, preferred_element_type=jnp.float32)
            else:
                placed = dot_first(unpack_t[b], rbuf[t].reshape(slots * n_b, PAIR))
            held[t, b * rows : (b + 1) * rows, :] = placed.astype(half)

    lane = lax.broadcasted_iota(jnp.int32, (1, PAIR), 1)

    def of_head(array, head):
        inside = (lane >= head * HEAD_DIM) & (lane < (head + 1) * HEAD_DIM)
        return jnp.where(inside, array, jnp.zeros_like(array))

    def attend(chunk, i):
        at = slice(i * rows, (i + 1) * rows)
        near = range(max(0, i - (n_b - 2)), min(n_b, i + n_b - 1))
        q_rows, d_rows = held[4 * chunk, at, :], held[4 * chunk + 3, at, :]
        q_scaled = (q_rows.astype(jnp.float32) * scale).astype(half)
        scene = plans[i, 2:3, :rows]
        same = {j: plans[j, 2:3, :rows] == scene for j in near}
        turned_grads = []
        add_k, add_v = {}, {}
        for head in range(2):
            d_head, q_head = of_head(d_rows, head), of_head(q_scaled, head)
            scores, weight_grad = {}, {}
            top = None
            for j in near:
                key_at = slice(j * rows, (j + 1) * rows)
                scores[j] = dot_last(held[4 * chunk + 1, key_at, :], q_head)
                weight_grad[j] = dot_last(held[4 * chunk + 2, key_at, :], d_head)
                high = jnp.where(same[j], jnp.max(scores[j], axis=0, keepdims=True), LOW_SCORE)
                top = high if top is None else jnp.maximum(top, high)
            total, dot = None, None
            weights = {}
            for j in near:
                weights[j] = jnp.exp(scores[j] - jnp.where(same[j], top, -LOW_SCORE))
                part = jnp.sum(weights[j], axis=0, keepdims=True)
                part_dot = jnp.sum(weights[j] * weight_grad[j], axis=0, keepdims=True)
                total = part if total is None else total + part
                dot = part_dot if dot is None else dot + part_dot
            inverse = 1.0 / total
            row_dot = dot * inverse
            turned_grad = None
            for j in near:
                key_at = slice(j * rows, (j + 1) * rows)
                normal = weights[j] * inverse
                score_half = (normal * (weight_grad[j] - row_dot)).astype(half)
                weight_half = normal.astype(half)
                key_t = held[4 * chunk + 1, key_at, :].T[head * HEAD_DIM : (head + 1) * HEAD_DIM, :]
                part = jnp.dot(key_t, score_half, preferred_element_type=jnp.float32)
                turned_grad = part if turned_grad is None else turned_grad + part
                part_k = jnp.dot(score_half, q_head, preferred_element_type=jnp.float32)
                part_v = jnp.dot(weight_half, d_head, preferred_element_type=jnp.float32)
                add_k[j] = part_k if head == 0 else add_k[j] + part_k
                add_v[j] = part_v if head == 0 else add_v[j] + part_v
            turned_grads.append(turned_grad * scale)
        for j in near:
            key_at = slice(j * rows, (j + 1) * rows)
            if i == max(0, j - (n_b - 2)):
                acc_k[key_at, :] = add_k[j]
                acc_v[key_at, :] = add_v[j]
            else:
                acc_k[key_at, :] += add_k[j]
                acc_v[key_at, :] += add_v[j]
        grads[3 * chunk, at, :] = jnp.concatenate(turned_grads, axis=0).T.astype(half)

    def back_pack(chunk, a):
        u = 3 * chunk + a
        if a == 1:
            grads[u] = acc_k[...].astype(half)
        if a == 2:
            grads[u] = acc_v[...].astype(half)
        if aligned:
            for b in range(n_b):
                packed = jnp.dot(
                    unpack_t[b], grads[u, b * rows : (b + 1) * rows, :], preferred_element_type=jnp.float32
                )
                back_s[u, :, :, b * cap : (b + 1) * cap] = packed.astype(half).reshape(n_g, n_b, cap, PAIR)
        else:
            packed = jnp.zeros((slots * n_b, PAIR), jnp.float32)
            for b in range(n_b):
                packed += jnp.dot(
                    unpack_t[b], grads[u, b * rows : (b + 1) * rows, :], preferred_element_type=jnp.float32
                )
            back_s[u] = packed.astype(half).reshape(n_g, n_b, n_b * cap, PAIR)
        for to in g_others:
            go(remote(back_s.at[u, to], back_r.at[u, g], bgs.at[u, to], bgr.at[u, g], (to, z)))
        back_r[u, g] = back_s[u, g]

    def back_middle(chunk, a):
        u = 3 * chunk + a
        for other in g_others:
            remote(
                back_s.at[u, other], back_r.at[u, other], bgs.at[u, other], bgr.at[u, other], (other, z)
            ).wait_recv()
        for b in range(n_b):
            came = back_r[u, :, b].reshape(slots, PAIR)
            back_z[u, b] = jnp.dot(pack_t[b], came, preferred_element_type=jnp.float32).astype(half)
        for to in z_others:
            go(remote(back_z.at[u, to], outs[a].at[:, columns(z, chunk)], bzs.at[u, to], bzr.at[u, z], (g, to)))
        pltpu.make_async_copy(back_z.at[u, z], outs[a].at[:, columns(z, chunk)], bzl.at[u]).start()

    def back_end(chunk, a):
        u = 3 * chunk + a
        pltpu.make_async_copy(back_z.at[u, z], outs[a].at[:, columns(z, chunk)], bzl.at[u]).wait()
        for other in z_others:
            remote(
                back_z.at[u, other],
                outs[a].at[:, columns(other, chunk)], bzs.at[u, other], bzr.at[u, other], (g, other),
            ).wait_recv()

    greet(n_g, n_b, g, z)
    for to in z_others:
        go(remote(plan_ref, plans.at[z], plan_s.at[to], plan_r.at[z], (g, to)))
    for t in range(min(DEPTH, steps)):
        start_z(t)
    plans[z] = plan_ref[...]
    for other in z_others:
        remote(plan_ref, plans.at[other], plan_s.at[other], plan_r.at[other], (g, other)).wait_recv()
    for b in range(n_b):
        hot = send_hot(plans[b], rows, slots)
        pack_t[b] = hot.astype(half)
        pack[b] = hot.T.astype(half)
        hot = take_hot(plans[b], rows, dims, b)
        unpack_t[b] = hot.astype(half)
        if aligned:
            unpack[b] = hot.T.astype(half)

    for t in range(steps):
        chunk, a = divmod(t, 4)
        if t + DEPTH < steps:
            start_z(t + DEPTH)
        pack_step(t)
        if t > 0:
            unpack_step(t - 1)
        if chunk > 0:
            for i in range(a * n_b // 4, (a + 1) * n_b // 4):
                attend(chunk - 1, i)
            if a == 3:
                for b in range(3):
                    back_pack(chunk - 1, b)
    unpack_step(steps - 1)
    last = chunks - 1
    waiting = [(c, a) for c in range(last) for a in range(3)]
    for i in range(n_b):
        attend(last, i)
        if waiting:
            back_middle(*waiting.pop(0))
    for a in range(3):
        back_pack(last, a)
    waiting += [(last, a) for a in range(3)]
    for c, a in waiting:
        back_middle(c, a)
    for c in range(chunks):
        for a in range(3):
            back_end(c, a)
    for copy in sends:
        copy.wait_send()


def shards(n_g, n_b, queries, keys, values, out_grad, send_rows, recv_slots, scene_frames):
    rows, features = queries.shape
    cap = send_rows.shape[2]
    dims = (n_g, n_b, cap)
    slots = n_g * n_b * cap
    chunks = features // n_b // PAIR
    long = max(slots, rows)
    plan = jnp.concatenate(
        [
            jnp.pad(send_rows.reshape(1, slots), ((0, 0), (0, long - slots))),
            jnp.pad(recv_slots, ((0, 0), (0, long - rows))),
            jnp.broadcast_to(scene_frames, (6, long)),
        ],
        axis=0,
    )
    in_vmem = pl.BlockSpec(memory_space=pltpu.VMEM)
    anywhere = pl.BlockSpec(memory_space=pl.ANY)
    group_rows = n_b * rows
    aligned = cap % 16 == 0
    taken = slots if aligned else slots * n_b
    half = jnp.bfloat16
    dma = pltpu.SemaphoreType.DMA
    out, back = 4 * chunks, 3 * chunks
    return tuple(
        pl.pallas_call(
            functools.partial(fused_kernel, dims),
            out_shape=[jax.ShapeDtypeStruct((rows, features), half)] * 3,
            in_specs=[in_vmem] + [anywhere] * 4,
            out_specs=[anywhere] * 3,
            scratch_shapes=[
                pltpu.VMEM((n_b, 8, long), jnp.int32),
                pltpu.VMEM((out, n_b, rows, PAIR), half),
                pltpu.VMEM((out, n_g, n_b, n_b * cap, PAIR), half),
                pltpu.VMEM((out, n_g, n_b, n_b * cap, PAIR), half),
                pltpu.VMEM((out, group_rows, PAIR), half),
                pltpu.VMEM((back, group_rows, PAIR), half),
                pltpu.VMEM((back, n_g, n_b, n_b * cap, PAIR), half),
                pltpu.VMEM((back, n_g, n_b, n_b * cap, PAIR), half),
                pltpu.VMEM((back, n_b, rows, PAIR), half),
                pltpu.VMEM((group_rows, PAIR), jnp.float32),
                pltpu.VMEM((group_rows, PAIR), jnp.float32),
                pltpu.VMEM((n_b, slots, rows), half),
                pltpu.VMEM((n_b, rows, slots) if aligned else (1, 16, 128), half),
                pltpu.VMEM((n_b, rows, slots), half),
                pltpu.VMEM((n_b, taken, rows), half),
                dma((n_b,)),
                dma((n_b,)),
                dma((out, n_b)),
                dma((out, n_b)),
                dma((out,)),
                dma((out, n_g)),
                dma((out, n_g)),
                dma((back, n_g)),
                dma((back, n_g)),
                dma((back, n_b)),
                dma((back, n_b)),
                dma((back,)),
            ],
            compiler_params=pltpu.CompilerParams(
                collective_id=0, has_side_effects=True, vmem_limit_bytes=VMEM_LIMIT
            ),
            name="fused",
        )(plan, queries, keys, values, out_grad)
    )


def solution(mesh):
    both = P(("group", "blk"), None)
    placed = (both, both, both, both, P(("group", "blk"), None, None), both, P("group", "blk"))
    return jax.shard_map(
        functools.partial(shards, mesh.shape["group"], mesh.shape["blk"]),
        mesh=mesh,
        in_specs=placed,
        out_specs=(both, both, both),
        check_vma=False,
    )
```

time: 681 us -> 125 us (0.18)
  waiting for transfers between devices: 380 us -> 0 us
  Pallas kernels: 0 us -> 118 us
  blocking collectives: 98.3 us -> 0 us
  local copies, waits for them, and re-layouts: 69.5 us -> 5.48 us
  other arithmetic: 43.5 us -> 0.67 us
  matrix products: 41.3 us -> 0 us
  starting transfers between devices: 31.9 us -> 0 us
  between operations: 15 us -> 1.31 us
    ppermute x20 -> x0, waiting for transfers between devices: 234 us -> none  [shifted(): return lax.ppermute(block, axis, route)]
    pallas_call x0 -> x1, Pallas kernels: none -> 118 us  [shards(): pl.pallas_call(functools.partial(fused_kernel, dims), out_shape=[jax.Shap...]
    all_to_all x3 -> x0, blocking collectives: 92.1 us -> none  [the longest x1 33.2 us: shards(): lax.all_to_all(pack_rows(values), ('group', 'blk'), split_axis=0, concat_...]
    all_to_all x4 -> x0, waiting for transfers between devices: 82.4 us -> none  [the longest x1 22.2 us: shards(): lax.all_to_all(unpack_rows(key_grad), ('group', 'blk'), split_axis=0, con...]
    all_gather x2 -> x0, waiting for transfers between devices: 62.2 us -> none  [the longest x1 31.2 us: shards(): key_piece = lax.all_gather(key_rows, 'blk', axis=0, tiled=True)]
    dot_general x22 -> x0, matrix products: 41.3 us -> none  [the longest x4 12.7 us: block_terms(): jnp.einsum('qhd,khd->hqk', grad_heads, value_heads, preferred_element_typ...]
    add x12 -> x0, other arithmetic: 26.9 us -> none  [the longest x4 9.24 us: cycle_block(): accums[1]]
    scatter x6 -> x0, local copies, waits for them, and re-layouts: 19.8 us -> none  [the longest x3 11 us: restore_rows(): return jnp.zeros((row_count, feature_width), jnp.bfloat16).at[send_plan.r...]
  transfers between devices with their start and end apart: 26 -> 0, of which waited for: 10 -> 0; matrix products, arithmetic and copies ran while one was open for 10% -> 0% of each run, Pallas kernels for 0% -> 0%
where the time goes in v2:
time: 125 us
  Pallas kernels  118 us (94%)
  local copies, waits for them, and re-layouts  5.48 us (4%)
  between operations  1.31 us (1%)
    pallas_call x1, Pallas kernels, shards(): pl.pallas_call(functools.partial(fused_kernel, dims), out_shape=[jax.Shap...  118 us
    unnamed x10, local copies, waits for them, and re-layouts  5.32 us

profile of v2, /device:TPU:1, one launch (start us, length us, event | category | flops | bytes accessed | tf_op | source)
XLA Modules:
  0.0 125.1 jit_solution(9239716319034232898)
XLA Ops:
  1.3 0.1 pad.7.clone
  1.4 0.8 copy.11
  2.1 0.0 copy-start.2
  2.1 0.1 reshape.9
  2.2 0.6 copy-done.2
  2.8 0.7 fusion.plan_ref
  3.5 117.7 %fused.1 = (bf16[256,1024]{1,0:T(8,128)(2,1)}, bf16[256,1024]{1,0:T(8,128)(2,1)}, bf16[256,1024]{1,0:T(8,128)(2,1)}) custom-call(s32[8,512]{1,0:T(8,128)} %fusion.plan_ref, bf16[256,1024]{1,0:T(8,128)(2,1)} %q.1, bf16[256,1024]{1,0:T(8,128)(2,1)} %k.1, bf16[256,1024]{1,0:T(8,128)(2,1)} %v.1, bf16[256,1024]{1,0:T(8,128)(2,1)} %d.1), custom_call_target="tpu_custom_call" | custom-call | tf_op jit(solution)/shard_map/fused/pallas_call | solution.py:306
  121.2 0.0 copy-start.1
  121.2 1.9 %copy.16 = bf16[256,1024]{1,0:T(8,128)(2,1)} copy(bf16[256,1024]{1,0:T(8,128)(2,1)} %get-tuple-element.6) | data formatting | bytes 1048576
  123.1 0.0 copy-done.1
  123.1 0.0 copy-start
  123.1 0.8 copy.17
  123.9 0.4 copy-done
  124.3 0.8 copy.18
  (1 shorter events, 0.0 us)
Async XLA Ops:
  2.1 0.7 copy-start.2
  121.2 1.9 %copy-start.1 = (bf16[256,1024]{1,0:T(8,128)(2,1)S(1)}, bf16[256,1024]{1,0:T(8,128)(2,1)}, u32[]{:S(2)}) copy-start(bf16[256,1024]{1,0:T(8,128)(2,1)} %get-tuple-element.7) | copy-start | bytes 1572868
  123.1 1.2 copy-start

commit v3 on v2

--- a/solution.py
+++ b/solution.py
@@ -11,7 +11,7 @@
 PAIR = 2 * HEAD_DIM
 MESH = pl.DeviceIdType.MESH
 LOW_SCORE = -1e30
-DEPTH = 3
+AHEAD = 1
 VMEM_LIMIT = 56 * 1024 * 1024
 
 
@@ -187,10 +187,6 @@
 
     def back_pack(chunk, a):
         u = 3 * chunk + a
-        if a == 1:
-            grads[u] = acc_k[...].astype(half)
-        if a == 2:
-            grads[u] = acc_v[...].astype(half)
         if aligned:
             for b in range(n_b):
                 packed = jnp.dot(
@@ -207,6 +203,9 @@
         for to in g_others:
             go(remote(back_s.at[u, to], back_r.at[u, g], bgs.at[u, to], bgr.at[u, g], (to, z)))
         back_r[u, g] = back_s[u, g]
+        if a == 0:
+            grads[u + 1] = acc_k[...].astype(half)
+            grads[u + 2] = acc_v[...].astype(half)
 
     def back_middle(chunk, a):
         u = 3 * chunk + a
@@ -230,10 +229,17 @@
                 outs[a].at[:, columns(other, chunk)], bzs.at[u, other], bzr.at[u, other], (g, other),
             ).wait_recv()
 
+    def back_rest(chunk):
+        back_pack(chunk, 1)
+        back_middle(chunk, 0)
+        back_pack(chunk, 2)
+        back_middle(chunk, 1)
+        back_middle(chunk, 2)
+
     greet(n_g, n_b, g, z)
     for to in z_others:
         go(remote(plan_ref, plans.at[z], plan_s.at[to], plan_r.at[z], (g, to)))
-    for t in range(min(DEPTH, steps)):
+    for t in range(AHEAD):
         start_z(t)
     plans[z] = plan_ref[...]
     for other in z_others:
@@ -247,10 +253,11 @@
         if aligned:
             unpack[b] = hot.T.astype(half)
 
+    last = chunks - 1
     for t in range(steps):
         chunk, a = divmod(t, 4)
-        if t + DEPTH < steps:
-            start_z(t + DEPTH)
+        if t + AHEAD < steps:
+            start_z(t + AHEAD)
         pack_step(t)
         if t > 0:
             unpack_step(t - 1)
@@ -258,20 +265,26 @@
             for i in range(a * n_b // 4, (a + 1) * n_b // 4):
                 attend(chunk - 1, i)
             if a == 3:
-                for b in range(3):
-                    back_pack(chunk - 1, b)
+                back_pack(chunk - 1, 0)
+        if chunk > 1 and a == 0:
+            back_rest(chunk - 2)
     unpack_step(steps - 1)
-    last = chunks - 1
-    waiting = [(c, a) for c in range(last) for a in range(3)]
-    for i in range(n_b):
-        attend(last, i)
-        if waiting:
-            back_middle(*waiting.pop(0))
-    for a in range(3):
-        back_pack(last, a)
-    waiting += [(last, a) for a in range(3)]
-    for c, a in waiting:
-        back_middle(c, a)
+    if chunks > 1:
+        back_pack(last - 1, 1)
+        attend(last, 0)
+        back_middle(last - 1, 0)
+        back_pack(last - 1, 2)
+        attend(last, 1)
+        back_middle(last - 1, 1)
+        for i in range(2, n_b):
+            attend(last, i)
+        back_pack(last, 0)
+        back_middle(last - 1, 2)
+    else:
+        for i in range(n_b):
+            attend(last, i)
+        back_pack(last, 0)
+    back_rest(last)
     for c in range(chunks):
         for a in range(3):
             back_end(c, a)

time: 125 us -> 119 us (0.952)
  Pallas kernels: 118 us -> 111 us
    pallas_call x1, Pallas kernels: 118 us -> 111 us  [shards(): pl.pallas_call(functools.partial(fused_kernel, dims), out_shape=[jax.Shap...]
where the time goes in v3:
time: 119 us
  Pallas kernels  111 us (93%)
  local copies, waits for them, and re-layouts  5.48 us (5%)
  between operations  1.31 us (1%)
    pallas_call x1, Pallas kernels, shards(): pl.pallas_call(functools.partial(fused_kernel, dims), out_shape=[jax.Shap...  111 us
    unnamed x10, local copies, waits for them, and re-layouts  5.32 us

profile of v3, /device:TPU:1, one launch (start us, length us, event | category | flops | bytes accessed | tf_op | source)
XLA Modules:
  0.0 118.6 jit_solution(790952348523286747)
XLA Ops:
  1.3 0.1 pad.7.clone
  1.4 0.8 copy.11
  2.1 0.0 copy-start.2
  2.1 0.1 reshape.9
  2.2 0.6 copy-done.2
  2.8 0.7 fusion.plan_ref
  3.5 111.2 %fused.1 = (bf16[256,1024]{1,0:T(8,128)(2,1)}, bf16[256,1024]{1,0:T(8,128)(2,1)}, bf16[256,1024]{1,0:T(8,128)(2,1)}) custom-call(s32[8,512]{1,0:T(8,128)} %fusion.plan_ref, bf16[256,1024]{1,0:T(8,128)(2,1)} %q.1, bf16[256,1024]{1,0:T(8,128)(2,1)} %k.1, bf16[256,1024]{1,0:T(8,128)(2,1)} %v.1, bf16[256,1024]{1,0:T(8,128)(2,1)} %d.1), custom_call_target="tpu_custom_call" | custom-call | tf_op jit(solution)/shard_map/fused/pallas_call | solution.py:319
  114.7 0.0 copy-start.1
  114.7 1.9 %copy.16 = bf16[256,1024]{1,0:T(8,128)(2,1)} copy(bf16[256,1024]{1,0:T(8,128)(2,1)} %get-tuple-element.6) | data formatting | bytes 1048576
  116.6 0.0 copy-done.1
  116.6 0.0 copy-start
  116.6 0.8 copy.17
  117.4 0.4 copy-done
  117.8 0.8 copy.18
  (1 shorter events, 0.0 us)
Async XLA Ops:
  2.1 0.7 copy-start.2
  114.7 1.9 %copy-start.1 = (bf16[256,1024]{1,0:T(8,128)(2,1)S(1)}, bf16[256,1024]{1,0:T(8,128)(2,1)}, u32[]{:S(2)}) copy-start(bf16[256,1024]{1,0:T(8,128)(2,1)} %get-tuple-element.7) | copy-start | bytes 1572868
  116.6 1.2 %copy-start = (bf16[256,1024]{1,0:T(8,128)(2,1)S(1)}, bf16[256,1024]{1,0:T(8,128)(2,1)}, u32[]{:S(2)}) copy-start(bf16[256,1024]{1,0:T(8,128)(2,1)} %get-tuple-element.8) | copy-start | bytes 1572868
